TPU v7x, 128 devices: a whole 4x4x4 slice. The times are simulated.
128 devices in a mesh: grp: 8 (over z_hi, x), mem: 16 (over z_lo, y, core).
Axes of the slice: x: 4, y: 4, z: 4 (z_hi: 2, z_lo: 2; z = z_hi * 2 + z_lo), core: 2. Of those that a mesh axis runs over, the one named last changes fastest.
Arguments:
- amplitudes: float32 [16384, 16384], P(('grp', 'mem')), may hold values from -6 to 6
- factors: float32 [16384, 1536], P('mem'), may hold values from -0.046875 to 0.046875
Outputs:
- cycle_term: float32 [16384, 16384], P(('grp', 'mem'))
All inputs are finite; a program needn't handle non-finite values.
Results may differ from a plain program's by a relative error of at most 0.000071.
Values sent between devices are 32-bit elements; how exact they have to be, the bound alone decides.
No kernel may reach another device: no remote copies, remote signals or barrier semaphores. Data moves between devices by JAX's collectives and lax.ppermute only.
A program may use at most 128 MiB of HBM per device.

v0:
```python
import jax
import jax.numpy as jnp
from jax import lax
from jax.sharding import PartitionSpec as P


def shards(amplitudes, factors):
    panels = lax.all_to_all(amplitudes, "mem", split_axis=1, concat_axis=0, tiled=True)
    members = lax.axis_size("mem")
    partial_fit = jnp.dot(
        panels, factors, precision=lax.Precision.HIGHEST, preferred_element_type=jnp.float32
    )
    fitted = lax.psum(partial_fit, "mem")
    cycle = jnp.dot(
        fitted, factors.T, precision=lax.Precision.HIGHEST, preferred_element_type=jnp.float32
    )
    owned = lax.all_to_all(cycle, "mem", split_axis=0, concat_axis=1, tiled=True)
    height = owned.shape[0]
    groups = lax.axis_size("grp")
    tiles = owned.reshape(height, groups * members, height)
    moved = lax.all_to_all(tiles, ("grp", "mem"), split_axis=1, concat_axis=1, tiled=True)
    mirrored = jnp.transpose(moved, (2, 1, 0)).reshape(height, owned.shape[1])
    return owned + mirrored


def solution(mesh):
    in_specs = (P(("grp", "mem"), None), P("mem", None))
    out_specs = P(("grp", "mem"), None)
    return jax.shard_map(shards, mesh=mesh, in_specs=in_specs, out_specs=out_specs, check_vma=False)
```

profile of v0, /device:TPU:6, one launch (start us, length us, event | category | flops | bytes accessed | tf_op | source)
XLA Modules:
  0.0 632.2 jit_solution(14595192972825952569)
XLA Ops:
  6.5 0.0 all-reduce.2.cloned.1.call-start
  6.5 9.0 %copy.6 = f32[128,16384]{0,1:T(8,128)} copy(f32[128,16384]{1,0:T(8,128)} %param.2) | data formatting | bytes 16777216 | tf_op args[0]
  15.5 101.2 %all_to_all.43 = f32[128,16,1024]{0,2,1:T(8,128)} all-to-all(f32[128,16,1024]{0,2,1:T(8,128)} %bitcast.19), channel_id=1, replica_groups=mesh['grp'=8,'mem'=16] {'mem'}, dimensions={1} | all-to-all | bytes 16777216 | tf_op jit(solution)/shard_map/all_to_all | solution.py:8
  116.7 9.2 %copy.7 = f32[16,128,1024]{2,1,0:T(8,128)} copy(f32[16,128,1024]{1,2,0:T(8,128)} %bitcast.18) | data formatting | bytes 16777216 | tf_op jit(solution)/shard_map/all_to_all | solution.py:8
  125.9 47.0 %fusion = f32[2048,1536]{1,0:T(8,128)} fusion(f32[2048,1024]{1,0:T(8,128)} %bitcast.21, f32[1024,1536]{1,0:T(8,128)} %param.3), kind=kOutput, calls=%fused_computation.1 | convolution fusion | flops 38654705664 | bytes 27262976 | tf_op jit(solution)/shard_map/dot_general | solution.py:10
  172.9 0.0 all-reduce.2.cloned.1.call-update
  172.9 158.3 %all-reduce.2.cloned.1.call-done = f32[2048,1536]{1,0:T(8,128)} async-done(((f32[2048,1536]{1,0:T(8,128)}), f32[2048,1536]{1,0:T(8,128)}) %all-reduce.2.cloned.1.call-update) | async-done | bytes 12582928 | tf_op jit(solution)/shard_map/psum | solution.py:13
  331.3 46.1 %fusion.1 = f32[2048,1024]{1,0:T(8,128)} fusion(f32[2048,1536]{1,0:T(8,128)} %all-reduce.2.cloned.1.call-done, f32[1024,1536]{1,0:T(8,128)} %param.3), kind=kOutput, calls=%fused_computation.2 | convolution fusion | flops 38654705664 | bytes 27262976 | tf_op jit(solution)/shard_map/dot_general | solution.py:14
  377.4 9.3 %copy.8 = f32[16,128,1024]{1,2,0:T(8,128)} copy(f32[16,128,1024]{2,1,0:T(8,128)} %bitcast.22) | data formatting | bytes 16777216 | tf_op jit(solution)/shard_map/all_to_all | solution.py:17
  386.7 98.9 %all_to_all.44 = f32[16,128,1024]{1,2,0:T(8,128)S(1)} all-to-all(f32[16,128,1024]{1,2,0:T(8,128)} %copy.8), channel_id=1, replica_groups=mesh['grp'=8,'mem'=16] {'mem'}, dimensions={0} | all-to-all | bytes 16777216 | tf_op jit(solution)/shard_map/all_to_all | solution.py:17
  485.6 0.0 copy-start
  485.6 112.0 %all_to_all.45 = f32[128,128,128]{0,2,1:T(8,128)} all-to-all(f32[128,128,128]{0,2,1:T(8,128)S(1)} %bitcast.17), channel_id=1, replica_groups=mesh['grp'=8,'mem'=16] {'grp','mem'}, dimensions={1} | all-to-all | bytes 16777216 | tf_op jit(solution)/shard_map/all_to_all | solution.py:21
  597.6 0.0 copy-done
  597.6 9.0 %copy.9 = f32[128,128,128]{0,2,1:T(8,128)} copy(f32[128,128,128]{2,0,1:T(8,128)} %bitcast.20) | data formatting | bytes 16777216 | tf_op jit(solution)/shard_map/transpose | solution.py:22
  606.6 9.7 %bitcast_add_fusion = f32[128,16384]{0,1:T(8,128)} fusion(f32[16,128,1024]{1,2,0:T(8,128)} %copy-done, f32[128,128,128]{0,2,1:T(8,128)} %copy.9), kind=kLoop, calls=%fused_computation | loop fusion | flops 2097152 | bytes 25165824 | tf_op jit(solution)/shard_map/add | solution.py:23
  616.4 9.0 %copy.10 = f32[128,16384]{1,0:T(8,128)} copy(f32[128,16384]{0,1:T(8,128)} %bitcast_add_fusion) | data formatting | bytes 16777216 | tf_op jit(solution)/shard_map/add | solution.py:23
Async XLA Ops:
  6.5 324.7 %all-reduce.2.cloned.1.call-start = ((), (), s32[]{:S(2)}) async-start(), calls=%async_computation.3 | async-start | bytes 25165824 | tf_op jit(solution)/shard_map/psum | solution.py:13
  485.6 112.0 %copy-start = (f32[16,128,1024]{1,2,0:T(8,128)}, f32[16,128,1024]{1,2,0:T(8,128)S(1)}, u32[]{:S(2)}) copy-start(f32[16,128,1024]{1,2,0:T(8,128)S(1)} %all_to_all.44) | copy-start | bytes 25165828
Sparse Core Ops, SparseCore 0:
  173.1 158.1 all-reduce.1
where the time goes:
time: 633 us; the launch traced here: 632 us
  blocking collectives  312 us (49%)
  waiting for transfers between devices  158 us (25%)
  matrix products  93.1 us (15%)
  local copies, waits for them, and re-layouts  45.5 us (7%)
  between operations  13.4 us (2%)
  other arithmetic  9.74 us (2%)
    psum x1, waiting for transfers between devices, shards(): fitted = lax.psum(partial_fit, 'mem')  158 us
    all_to_all x1, blocking collectives, shards(): lax.all_to_all(tiles, ('grp', 'mem'), split_axis=1, concat_axis=1, tiled=...  112 us
    all_to_all x1, blocking collectives, shards(): lax.all_to_all(amplitudes, 'mem', split_axis=1, concat_axis=0, tiled=True)  101 us
    all_to_all x1, blocking collectives, shards(): lax.all_to_all(cycle, 'mem', split_axis=0, concat_axis=1, tiled=True)  98.9 us
    dot_general x1, matrix products, shards(): jnp.dot(panels, factors, precision=lax.Precision.HIGHEST, preferred_eleme...  47 us
    dot_general x1, matrix products, shards(): jnp.dot(fitted, factors.T, precision=lax.Precision.HIGHEST, preferred_ele...  46.1 us
  transfers between devices with their start and end apart: 1, of which 1 were waited for; matrix products, arithmetic and copies ran while one was open for 0% of the time, Pallas kernels for 0%

commit v1 on v0

v1 whole, which is shorter than its diff:
```python
import functools

import jax
import jax.numpy as jnp
import numpy as np
from jax import lax
from jax.experimental import pallas as pl
from jax.experimental.pallas import tpu as pltpu
from jax.sharding import Mesh
from jax.sharding import PartitionSpec as P

SIZES = (2, 4, 2, 4, 2)
ALL = ("zh", "x", "zl", "y", "c")
MEM = ("zl", "y", "c")


def permutation(move):
    pairs = []
    for source in range(int(np.prod(SIZES))):
        zh, x, zl, y, c = (int(i) for i in np.unravel_index(source, SIZES))
        tx, ty, tz, tc = move(x, y, 2 * zh + zl, c)
        tx, ty, tz, tc = tx % 4, ty % 4, tz % 4, tc % 2
        pairs.append((source, int(np.ravel_multi_index((tz // 2, tx, tz % 2, ty, tc), SIZES))))
    return pairs


ALONG_X = permutation(lambda x, y, z, c: (x + 1 - 2 * c, y, z, c))
ALONG_Y = permutation(lambda x, y, z, c: (x, y + 1 - 2 * c, z, c))
ALONG_Z = permutation(lambda x, y, z, c: (x, y, z + 1 - 2 * c, c))
CORES = permutation(lambda x, y, z, c: (x, y, z, c + 1))

ROUNDS = (
    ((ALONG_Y, "a00", "a01"), (ALONG_Z, "a00", "a10")),
    ((ALONG_X, "a01", "b01"), (ALONG_Y, "a01", "a02"), (ALONG_Z, "b00", "b10")),
    ((ALONG_X, "a02", "b02"), (ALONG_Y, "a02", "a03"), (ALONG_Z, "a01", "a11")),
    ((ALONG_X, "a03", "b03"), (ALONG_Y, "b10", "b11"), (ALONG_Z, "a03", "a13")),
    ((ALONG_X, "a13", "b13"), (ALONG_Y, "b11", "b12"), (ALONG_Z, "a02", "a12")),
)


PIECES = ["a00", "b00"] + [target for moves in ROUNDS for _, _, target in moves]
SLOTS = 3
NT = (((1,), (1,)), ((), ()))


def dot(a, b):
    return jnp.dot(a, b, precision=lax.Precision.HIGH, preferred_element_type=jnp.float32)


def parts(value):
    high = value.astype(jnp.bfloat16)
    return high, (value - high.astype(jnp.float32)).astype(jnp.bfloat16)


def cycle_kernel(
    rows, mine_at, theirs_at, fitted, *refs
):
    pieces, (owned, other, high, low, held, tiles, in_sems, out_sems) = refs[:-8], refs[-8:]
    count = len(pieces)
    half = pieces[0].shape[0]
    width = min(2 * rows, half)
    per_step = width // rows
    steps = half // width
    high[...], low[...] = parts(fitted[...])

    def fetch(i):
        return pltpu.make_async_copy(pieces[i], held.at[i % SLOTS], in_sems.at[i % SLOTS])

    def drain(i):
        at = pl.ds(mine_at[i], half // rows)
        there = pl.ds(theirs_at[i], half // rows)
        slot = i % 2
        return (
            pltpu.make_async_copy(tiles.at[slot, 0], owned.at[at], out_sems.at[slot, 0]),
            pltpu.make_async_copy(tiles.at[slot, 1], other.at[there], out_sems.at[slot, 1]),
        )

    for i in range(min(SLOTS - 1, count)):
        fetch(i).start()
    for i in range(count):
        if i + SLOTS - 1 < count:
            fetch(i + SLOTS - 1).start()
        fetch(i).wait()
        if i >= 2:
            for copy in drain(i - 2):
                copy.wait()
        for step in range(steps):
            piece_high, piece_low = parts(held[i % SLOTS, step * width : (step + 1) * width])
            product = functools.partial(
                lax.dot_general, dimension_numbers=NT, preferred_element_type=jnp.float32
            )
            total = (
                product(low[...], piece_high) + product(high[...], piece_low)
            ) + product(high[...], piece_high)
            for k in range(per_step):
                for who in range(2):
                    tiles[i % 2, who, step * per_step + k] = total[
                        who * rows : (who + 1) * rows, k * rows : (k + 1) * rows
                    ]
        for copy in drain(i):
            copy.start()
    for i in range(max(count - 2, 0), count):
        for copy in drain(i):
            copy.wait()


def make_cycle(rows, mine_at, theirs_at, fitted, pieces):
    half, depth = pieces[0].shape
    total = len(pieces) * half // rows
    flops = 3 * 2 * fitted.shape[0] * half * depth * len(pieces)
    smem = pl.BlockSpec(memory_space=pltpu.SMEM)
    anywhere = pl.BlockSpec(memory_space=pl.ANY)
    return pl.pallas_call(
        functools.partial(cycle_kernel, rows),
        out_shape=(
            jax.ShapeDtypeStruct((2 * total, rows, rows), jnp.float32),
            jax.ShapeDtypeStruct((total, rows, rows), jnp.float32),
        ),
        in_specs=[smem, smem, pl.BlockSpec(memory_space=pltpu.VMEM)] + [anywhere] * len(pieces),
        out_specs=(anywhere, anywhere),
        scratch_shapes=[
            pltpu.VMEM(fitted.shape, jnp.bfloat16),
            pltpu.VMEM(fitted.shape, jnp.bfloat16),
            pltpu.VMEM((SLOTS, half, depth), jnp.float32),
            pltpu.VMEM((2, 2, half // rows, rows, rows), jnp.float32),
            pltpu.SemaphoreType.DMA((SLOTS,)),
            pltpu.SemaphoreType.DMA((2, 2)),
        ],
        cost_estimate=pl.CostEstimate(
            flops=flops, bytes_accessed=4 * len(pieces) * half * (depth + 2 * rows), transcendentals=0
        ),
        compiler_params=pltpu.CompilerParams(vmem_limit_bytes=40 * 2**20),
        name="cycle",
    )(mine_at, theirs_at, fitted, *pieces)


def join_kernel(straight, mirrored, out):
    rows = straight.shape[1]
    for k in range(straight.shape[0]):
        out[:, k * rows : (k + 1) * rows] = straight[k] + mirrored[k].T


def join(straight, mirrored):
    count, rows, _ = straight.shape
    group = 16
    tile = pl.BlockSpec((group, rows, rows), lambda i: (i, 0, 0))
    return pl.pallas_call(
        join_kernel,
        grid=(count // group,),
        out_shape=jax.ShapeDtypeStruct((rows, count * rows), jnp.float32),
        in_specs=[tile, tile],
        out_specs=pl.BlockSpec((rows, group * rows), lambda i: (0, i)),
        compiler_params=pltpu.CompilerParams(vmem_limit_bytes=32 * 2**20),
        name="join",
    )(straight, mirrored)


def shards(amplitudes, factors):
    rows = amplitudes.shape[0]
    block = factors.shape[0]
    half = block // 2
    core = lax.axis_index("c")
    parity = lax.axis_index("x") & 1

    def place(piece):
        first = parity if piece[0] == "a" else 1 - parity
        z = lax.axis_index("zl") ^ int(piece[1])
        y = (lax.axis_index("y") + (2 * core - 1) * int(piece[2])) & 3
        return 4 * z + y, first * half

    pieces = {
        "a00": lax.dynamic_slice_in_dim(factors, parity * half, half, 0),
        "b00": lax.dynamic_slice_in_dim(factors, (1 - parity) * half, half, 0),
    }

    def columns(wanted):
        return jnp.stack(
            [lax.dynamic_slice_in_dim(amplitudes, (2 * i + wanted) * block, block, 1) for i in range(8)]
        )

    theirs = lax.ppermute(columns(1 - core), ALL, CORES)
    both = jnp.concatenate([columns(core), theirs], axis=1)

    def multiply(name):
        at, offset = place(name)
        left = lax.dynamic_slice(both, (at, 0, offset), (1, 2 * rows, half))[0]
        return dot(left, pieces[name])

    def take(names, fitted):
        for name in names:
            term = multiply(name)
            fitted = term if fitted is None else fitted + term
        return fitted

    fitted = None
    ready = ["a00", "b00"]
    for moves in ROUNDS:
        sources = lax.optimization_barrier([pieces[source] for _, source, _ in moves])
        arrived = [lax.ppermute(value, ALL, route) for value, (route, _, _) in zip(sources, moves)]
        fitted = take(ready, fitted)
        arrived = lax.optimization_barrier(arrived)
        for value, (_, _, target) in zip(arrived, moves):
            pieces[target] = value
        ready = [target for _, _, target in moves]
    fitted = take(ready, fitted)

    swapped = lax.ppermute(fitted, ALL, CORES)
    fitted = fitted + jnp.concatenate([swapped[rows:], swapped[:rows]], axis=0)
    places = [place(name) for name in PIECES]
    group = block // rows
    mine_at = jnp.stack([(2 * at + core) * group + offset // rows for at, offset in places])
    theirs_at = jnp.stack([at * group + offset // rows for at, offset in places])
    owned, other = make_cycle(rows, mine_at, theirs_at, fitted, [pieces[name] for name in PIECES])
    other = lax.ppermute(other, ALL, CORES)
    owned = lax.dynamic_update_slice(
        owned.reshape(8, 2, group, rows, rows),
        other.reshape(8, 1, group, rows, rows),
        (0, 1 - core, 0, 0, 0),
    ).reshape(-1, rows, rows)
    moved = lax.all_to_all(owned, ALL, split_axis=0, concat_axis=0, tiled=True)
    return join(owned, moved)


def solution(mesh):
    mesh = Mesh(mesh.devices.reshape(SIZES), ALL)
    in_specs = (P(ALL, None), P(MEM, None))
    return jax.shard_map(
        shards, mesh=mesh, in_specs=in_specs, out_specs=P(ALL, None), check_vma=False
    )
```

time: 633 us -> 402 us (0.64)
  blocking collectives: 312 us -> 114 us
  Pallas kernels: 0 us -> 31.9 us
  matrix products: 93.1 us -> 65.5 us
  local copies, waits for them, and re-layouts: 45.5 us -> 25.8 us
  waiting for transfers between devices: 158 us -> 142 us
  starting transfers between devices: 0.01 us -> 13.5 us
  between operations: 13.4 us -> 0.69 us
  other arithmetic: 9.74 us -> 1.6 us
    all_to_all x3 -> x1, blocking collectives: 312 us -> 114 us  [shards(): moved = lax.all_to_all(owned, ALL, split_axis=0, concat_axis=0, tiled=True)]
    psum x1 -> x0, waiting for transfers between devices: 158 us -> none  [shards(): fitted = lax.psum(partial_fit, 'mem')]
    ppermute x0 -> x17, waiting for transfers between devices: none -> 142 us  [the longest x14 131 us: shards(): lax.ppermute(value, ALL, route)]
    pallas_call x0 -> x2, Pallas kernels: none -> 31.9 us  [the longest x1 26.4 us: make_cycle(): pl.pallas_call(functools.partial(cycle_kernel, rows), out_shape=(jax.Shap...]
    dot_general x2 -> x16, matrix products: 93.1 us -> 65.5 us  [dot(): jnp.dot(a, b, precision=lax.Precision.HIGH, preferred_element_type=jnp.fl...]
    all_to_all x2 -> x0, local copies, waits for them, and re-layouts: 18.5 us -> none  [the longest x1 9.25 us: shards(): lax.all_to_all(cycle, 'mem', split_axis=0, concat_axis=1, tiled=True)]
    ppermute x0 -> x17, starting transfers between devices: none -> 13.5 us  [the longest x14 13.3 us: shards(): lax.ppermute(value, ALL, route)]
    transpose x1 -> x0, local copies, waits for them, and re-layouts: 8.99 us -> none  [shards(): mirrored = jnp.transpose(moved, (2, 1, 0)).reshape(height, owned.shape[1])]
  transfers between devices with their start and end apart: 1 -> 17, of which waited for: 1 -> 14; matrix products, arithmetic and copies ran while one was open for 0% -> 15% of each run, Pallas kernels for 0% -> 0%
where the time goes in v1:
time: 402 us; the launch traced here: 395 us
  waiting for transfers between devices  142 us (35%)
  blocking collectives  114 us (28%)
  matrix products  65.5 us (16%)
  Pallas kernels  31.9 us (8%)
  local copies, waits for them, and re-layouts  25.8 us (6%)
  starting transfers between devices  13.5 us (3%)
    ppermute x14, waiting for transfers between devices, shards(): lax.ppermute(value, ALL, route)  131 us
    all_to_all x1, blocking collectives, shards(): moved = lax.all_to_all(owned, ALL, split_axis=0, concat_axis=0, tiled=True)  114 us
    dot_general x16, matrix products, dot(): jnp.dot(a, b, precision=lax.Precision.HIGH, preferred_element_type=jnp.fl...  65.5 us
    pallas_call x1, Pallas kernels, make_cycle(): pl.pallas_call(functools.partial(cycle_kernel, rows), out_shape=(jax.Shap...  26.4 us
    unnamed x35, local copies, waits for them, and re-layouts  15 us
    ppermute x14, starting transfers between devices, shards(): lax.ppermute(value, ALL, route)  13.3 us
  transfers between devices with their start and end apart: 17, of which 14 were waited for; matrix products, arithmetic and copies ran while one was open for 15% of the time, Pallas kernels for 0%

profile of v1, /device:TPU:6, one launch (start us, length us, event | category | flops | bytes accessed | tf_op | source)
XLA Modules:
  0.0 394.9 jit_solution(11340510282339044807)
XLA Ops:
  0.0 3.3 constant_dynamic-slice_fusion
  8.6 33.4 %collective-permute-done.1.refs_2_ = f32[512,1536]{1,0:T(8,128)} collective-permute-done((f32[512,1536]{1,0:T(8,128)S(1)}, f32[512,1536]{1,0:T(8,128)}, u32[]{:S(2)}, u32[]{:S(2)}) %collective-permute-start.1) | collective-permute-done | bytes 3145760 | tf_op jit(solution)/shard_map/ppermute | solution.py:199
  46.3 35.4 %collective-permute-done.3.refs_4_ = f32[512,1536]{1,0:T(8,128)S(1)} collective-permute-done((f32[512,1536]{1,0:T(8,128)}, f32[512,1536]{1,0:T(8,128)S(1)}, u32[]{:S(2)}, u32[]{:S(2)}) %collective-permute-start.3) | collective-permute-done | bytes 3145760 | tf_op jit(solution)/shard_map/ppermute | solution.py:199
  87.7 2.4 bitcast_dynamic-update-slice_fusion.7
  90.1 3.0 bitcast_dynamic-update-slice_fusion.6
  95.3 2.3 bitcast_dynamic-update-slice_fusion.4
  102.0 20.4 %collective-permute-done.6.refs_7_ = f32[512,1536]{1,0:T(8,128)} collective-permute-done((f32[512,1536]{1,0:T(8,128)}, f32[512,1536]{1,0:T(8,128)}, u32[]{:S(2)}, u32[]{:S(2)}) %collective-permute-start.6) | collective-permute-done | bytes 3145760 | tf_op jit(solution)/shard_map/ppermute | solution.py:199
  122.5 2.7 collective-permute-done.7.refs_8_
  128.2 3.8 fusion.56
  132.0 3.0 fusion.54
  134.9 29.1 %collective-permute-done.9.refs_10_ = f32[512,1536]{1,0:T(8,128)} collective-permute-done((f32[512,1536]{1,0:T(8,128)}, f32[512,1536]{1,0:T(8,128)}, u32[]{:S(2)}, u32[]{:S(2)}) %collective-permute-start.9) | collective-permute-done | bytes 3145760 | tf_op jit(solution)/shard_map/ppermute | solution.py:199
  164.0 2.7 collective-permute-done.10.refs_11_
  170.2 2.8 fusion.58
  173.0 3.8 fusion.48
  176.8 2.8 fusion.52
  179.6 3.6 fusion.50
  183.2 3.6 fusion.46
  186.9 3.6 fusion.44
  190.5 3.6 fusion.42
  194.1 4.8 %fusion.38 = f32[256,1536]{1,0:T(8,128)} fusion(f32[512,1536]{1,0:T(8,128)} %collective-permute-done.10.refs_11_, s32[]{:T(128)S(6)} %select_n.168, s32[]{:T(128)S(6)} %select_n.163, f32[8,128,1024]{2,1,0:T(8,128)} %get-tuple-element.66, f32[8,128,1024]{2,1,0:T(8,128)} %collective-permute-done), kind=kOutput, calls=%fused_computation.72 | convolution fusion | flops 1208090624 | bytes 13107208 | tf_op jit(solution)/shard_map/dot_general | solution.py:47
  199.0 5.0 %fusion.40 = f32[256,1536]{1,0:T(8,128)} fusion(f32[512,1536]{1,0:T(8,128)} %collective-permute-done.9.refs_10_, s32[]{:T(128)S(6)} %select_n.167, s32[]{:T(128)S(6)} %select_n.163, f32[8,128,1024]{2,1,0:T(8,128)} %get-tuple-element.66, f32[8,128,1024]{2,1,0:T(8,128)} %collective-permute-done), kind=kOutput, calls=%fused_computation.74 | convolution fusion | flops 1208090624 | bytes 13107208 | tf_op jit(solution)/shard_map/dot_general | solution.py:47
  204.0 4.8 %fusion.36 = f32[256,1536]{1,0:T(8,128)} fusion(f32[512,1536]{1,0:T(8,128)} %collective-permute-done.11.refs_12_, s32[]{:T(128)S(6)} %select_n.169, s32[]{:T(128)S(6)} %select_n.162, f32[8,128,1024]{2,1,0:T(8,128)} %get-tuple-element.66, f32[8,128,1024]{2,1,0:T(8,128)} %collective-permute-done), kind=kOutput, calls=%fused_computation.70 | convolution fusion | flops 1208090624 | bytes 13107208 | tf_op jit(solution)/shard_map/dot_general | solution.py:47
  208.9 4.4 %fusion.34 = f32[256,1536]{1,0:T(8,128)} fusion(f32[512,1536]{1,0:T(8,128)S(1)} %collective-permute-done.12.refs_13_, s32[]{:T(128)S(6)} %select_n.169, s32[]{:T(128)S(6)} %select_n.163, f32[8,128,1024]{2,1,0:T(8,128)} %get-tuple-element.66, f32[8,128,1024]{2,1,0:T(8,128)} %collective-permute-done), kind=kOutput, calls=%fused_computation.68 | convolution fusion | flops 1208090624 | bytes 13107208 | tf_op jit(solution)/shard_map/dot_general | solution.py:47
  213.2 3.9 fusion.32
  217.2 3.9 fusion.30
  221.1 8.1 %fusion.13 = f32[256,1536]{1,0:T(8,128)} fusion(f32[256,1536]{1,0:T(8,128)} %fusion.30, f32[256,1536]{1,0:T(8,128)} %fusion.32, f32[256,1536]{1,0:T(8,128)} %fusion.34, f32[256,1536]{1,0:T(8,128)} %fusion.36, f32[256,1536]{1,0:T(8,128)} %fusion.38, f32[256,1536]{1,0:T(8,128)} %fusion.40, f32[256,1536]{1,0:T(8,128)S(1)} %fusion.42, ...), kind=kOutput, calls=%fused_computation.46 | convolution fusion | flops 1213988864 | bytes 36701696 | tf_op jit(solution)/shard_map/dot_general | solution.py:47
  229.4 3.5 collective-permute-done.15
  236.0 26.4 %cycle.1 = (f32[128,128,128]{2,1,0:T(8,128)}, f32[64,128,128]{2,1,0:T(8,128)}) custom-call(s32[16]{0:T(128)S(1)} %stack.172.mine_at, s32[16]{0:T(128)S(1)} %stack.189.theirs_at, f32[256,1536]{1,0:T(8,128)S(1)} %maximum_add_fusion.fitted, f32[512,1536]{1,0:T(8,128)S(1)} %copy-done.2, f32[512,1536]{1,0:T(8,128)S(1)} %get-tuple-element.41.refs_1_, ...), custom_call_target="tpu_custom_call" | custom-call | flops 19327352832 | bytes 58720256 | tf_op jit(solution)/shard_map/cycle/pallas_call | solution.py:113
  262.6 7.4 %collective-permute-done.16 = f32[64,128,128]{2,1,0:T(8,128)} collective-permute-done((f32[64,128,128]{2,1,0:T(8,128)}, f32[64,128,128]{2,1,0:T(8,128)}, u32[]{:S(2)}, u32[]{:S(2)}) %collective-permute-start.16) | collective-permute-done | bytes 4194336 | tf_op jit(solution)/shard_map/ppermute | solution.py:214
  270.0 4.7 %constant_dynamic-update-slice_fusion = f32[8,2,8,128,128]{4,3,2,1,0:T(8,128)} fusion(f32[8,2,8,128,128]{4,3,2,1,0:T(8,128)} %bitcast.131, f32[8,1,8,128,128]{4,3,2,1,0:T(8,128)} %bitcast.66, s32[]{:T(128)S(6)} %select_n.171), kind=kLoop, calls=%fused_computation.111 | loop fusion | bytes 8388612 | tf_op jit(solution)/shard_map/dynamic_update_slice | solution.py:215
  274.7 114.2 %all_to_all.5.mirrored = f32[128,128,128]{2,1,0:T(8,128)S(1)} all-to-all(f32[128,128,128]{2,1,0:T(8,128)} %bitcast.132), channel_id=1, replica_groups=mesh['zh'=2,'x'=4,'zl'=2,'y'=4,'c'=2] {'zh','x','zl','y','c'}, dimensions={0} | all-to-all | bytes 16777216 | tf_op jit(solution)/shard_map/all_to_all | solution.py:220
  388.9 5.6 %join.1 = f32[128,16384]{1,0:T(8,128)} custom-call(f32[128,128,128]{2,1,0:T(8,128)S(1)} %bitcast.133, f32[128,128,128]{2,1,0:T(8,128)S(1)} %all_to_all.5.mirrored), custom_call_target="tpu_custom_call" | custom-call | tf_op jit(solution)/shard_map/join/pallas_call | solution.py:147
  (64 shorter events, 32.3 us)
Async XLA Ops:
  3.3 38.7 %collective-permute-start.1 = (f32[512,1536]{1,0:T(8,128)S(1)}, f32[512,1536]{1,0:T(8,128)}, u32[]{:S(2)}, u32[]{:S(2)}) collective-permute-start(f32[512,1536]{1,0:T(8,128)S(1)} %get-tuple-element.36.refs_0_), channel_id=1, source_target_pairs={{0,2},{1,7},{2,4},{3,1},{4,6},{5,3},{6,0},{7,5},{8,10},{9,15},{10,... | collective-permute-start | bytes 9437192 | tf_op jit(solution)/shard_map/ppermute | solution.py:199
  4.9 39.3 %collective-permute-start.2 = (f32[512,1536]{1,0:T(8,128)S(1)}, f32[512,1536]{1,0:T(8,128)S(1)}, u32[]{:S(2)}, u32[]{:S(2)}) collective-permute-start(f32[512,1536]{1,0:T(8,128)S(1)} %get-tuple-element.36.refs_0_), channel_id=1, source_target_pairs={{0,8},{1,73},{2,10},{3,75},{4,12},{5,77},{6,14},{7,79},{8,64},{9,1... | collective-permute-start | bytes 9437192 | tf_op jit(solution)/shard_map/ppermute | solution.py:199
  6.9 1.7 copy-start.1
  44.2 40.6 %copy-start.3 = (f32[512,1536]{1,0:T(8,128)}, f32[512,1536]{1,0:T(8,128)S(1)}, u32[]{:S(2)}) copy-start(f32[512,1536]{1,0:T(8,128)S(1)} %collective-permute-done.2.refs_3_) | copy-start | bytes 9437188
  44.2 37.5 %collective-permute-start.3 = (f32[512,1536]{1,0:T(8,128)}, f32[512,1536]{1,0:T(8,128)S(1)}, u32[]{:S(2)}, u32[]{:S(2)}) collective-permute-start(f32[512,1536]{1,0:T(8,128)} %collective-permute-done.1.refs_2_), channel_id=1, source_target_pairs={{0,16},{1,49},{2,18},{3,51},{4,20},{5,53},{6,22},{7,55},{8,24},{9,... | collective-permute-start | bytes 9437192 | tf_op jit(solution)/shard_map/ppermute | solution.py:199
  44.7 38.8 %collective-permute-start.4 = (f32[512,1536]{1,0:T(8,128)}, f32[512,1536]{1,0:T(8,128)}, u32[]{:S(2)}, u32[]{:S(2)}) collective-permute-start(f32[512,1536]{1,0:T(8,128)} %collective-permute-done.1.refs_2_), channel_id=1, source_target_pairs={{0,2},{1,7},{2,4},{3,1},{4,6},{5,3},{6,0},{7,5},{8,10},{9,15},{10,... | collective-permute-start | bytes 9437192 | tf_op jit(solution)/shard_map/ppermute | solution.py:199
  46.3 38.6 %collective-permute-start.5 = (f32[512,1536]{1,0:T(8,128)S(1)}, f32[512,1536]{1,0:T(8,128)}, u32[]{:S(2)}, u32[]{:S(2)}) collective-permute-start(f32[512,1536]{1,0:T(8,128)S(1)} %get-tuple-element.41.refs_1_), channel_id=1, source_target_pairs={{0,8},{1,73},{2,10},{3,75},{4,12},{5,77},{6,14},{7,79},{8,64},{9,1... | collective-permute-start | bytes 9437192 | tf_op jit(solution)/shard_map/ppermute | solution.py:199
  81.7 4.7 %copy-start.7 = (f32[512,1536]{1,0:T(8,128)}, f32[512,1536]{1,0:T(8,128)S(1)}, u32[]{:S(2)}) copy-start(f32[512,1536]{1,0:T(8,128)S(1)} %collective-permute-done.3.refs_4_) | copy-start | bytes 9437188
  84.9 37.6 %collective-permute-start.6 = (f32[512,1536]{1,0:T(8,128)}, f32[512,1536]{1,0:T(8,128)}, u32[]{:S(2)}, u32[]{:S(2)}) collective-permute-start(f32[512,1536]{1,0:T(8,128)} %collective-permute-done.4.refs_5_), channel_id=1, source_target_pairs={{0,16},{1,49},{2,18},{3,51},{4,20},{5,53},{6,22},{7,55},{8,24},{9,... | collective-permute-start | bytes 9437192 | tf_op jit(solution)/shard_map/ppermute | solution.py:199
  86.4 38.8 %collective-permute-start.7 = (f32[512,1536]{1,0:T(8,128)}, f32[512,1536]{1,0:T(8,128)}, u32[]{:S(2)}, u32[]{:S(2)}) collective-permute-start(f32[512,1536]{1,0:T(8,128)} %collective-permute-done.4.refs_5_), channel_id=1, source_target_pairs={{0,2},{1,7},{2,4},{3,1},{4,6},{5,3},{6,0},{7,5},{8,10},{9,15},{10,... | collective-permute-start | bytes 9437192 | tf_op jit(solution)/shard_map/ppermute | solution.py:199
  87.6 38.8 %collective-permute-start.8 = (f32[512,1536]{1,0:T(8,128)}, f32[512,1536]{1,0:T(8,128)}, u32[]{:S(2)}, u32[]{:S(2)}) collective-permute-start(f32[512,1536]{1,0:T(8,128)} %collective-permute-done.1.refs_2_), channel_id=1, source_target_pairs={{0,8},{1,73},{2,10},{3,75},{4,12},{5,77},{6,14},{7,79},{8,64},{9,1... | collective-permute-start | bytes 9437192 | tf_op jit(solution)/shard_map/ppermute | solution.py:199
  87.6 10.0 %copy-start.6 = (f32[128,16384]{1,0:T(8,128)S(1)}, f32[128,16384]{1,0:T(8,128)}, u32[]{:S(2)}) copy-start(f32[128,16384]{1,0:T(8,128)} %param.2) | copy-start | bytes 25165828
  102.0 26.1 %collective-permute-start = (f32[8,128,1024]{2,1,0:T(8,128)}, f32[8,128,1024]{2,1,0:T(8,128)}, u32[]{:S(2)}, u32[]{:S(2)}) collective-permute-start(f32[8,128,1024]{2,1,0:T(8,128)} %get-tuple-element.65), channel_id=1, source_target_pairs={{0,1},{1,0},{2,3},{3,2},{4,5},{5,4},{6,7},{7,6},{8,9},{9,8},{10,11... | collective-permute-start | bytes 12582920 | tf_op jit(solution)/shard_map/ppermute | solution.py:181
  126.4 37.6 %collective-permute-start.9 = (f32[512,1536]{1,0:T(8,128)}, f32[512,1536]{1,0:T(8,128)}, u32[]{:S(2)}, u32[]{:S(2)}) collective-permute-start(f32[512,1536]{1,0:T(8,128)} %collective-permute-done.7.refs_8_), channel_id=1, source_target_pairs={{0,16},{1,49},{2,18},{3,51},{4,20},{5,53},{6,22},{7,55},{8,24},{9,... | collective-permute-start | bytes 9437192 | tf_op jit(solution)/shard_map/ppermute | solution.py:199
  127.9 38.8 %collective-permute-start.10 = (f32[512,1536]{1,0:T(8,128)}, f32[512,1536]{1,0:T(8,128)}, u32[]{:S(2)}, u32[]{:S(2)}) collective-permute-start(f32[512,1536]{1,0:T(8,128)} %collective-permute-done.5.refs_6_), channel_id=1, source_target_pairs={{0,2},{1,7},{2,4},{3,1},{4,6},{5,3},{6,0},{7,5},{8,10},{9,15},{10,... | collective-permute-start | bytes 9437192 | tf_op jit(solution)/shard_map/ppermute | solution.py:199
  128.2 38.8 %collective-permute-start.11 = (f32[512,1536]{1,0:T(8,128)}, f32[512,1536]{1,0:T(8,128)}, u32[]{:S(2)}, u32[]{:S(2)}) collective-permute-start(f32[512,1536]{1,0:T(8,128)} %collective-permute-done.7.refs_8_), channel_id=1, source_target_pairs={{0,8},{1,73},{2,10},{3,75},{4,12},{5,77},{6,14},{7,79},{8,64},{9,1... | collective-permute-start | bytes 9437192 | tf_op jit(solution)/shard_map/ppermute | solution.py:199
  128.2 3.8 copy-start.4
  128.2 42.0 %slice-start = ((s8[6291456]{0:T(1024)(128)(4,1)}), s8[4194304]{0:T(1024)(128)(4,1)S(1)}, s32[]{:S(2)}) async-start(s8[6291456]{0:T(1024)(128)(4,1)} %bitcast.134), calls=%async_computation.1 | async-start | bytes 8388608
  132.0 38.2 %slice-start.1 = ((s8[6291456]{0:T(1024)(128)(4,1)}), s8[2097152]{0:T(1024)(128)(4,1)S(1)}, s32[]{:S(2)}) async-start(s8[6291456]{0:T(1024)(128)(4,1)} %bitcast.134), calls=%async_computation.2 | async-start | bytes 4194304
  167.0 41.8 %collective-permute-start.12 = (f32[512,1536]{1,0:T(8,128)}, f32[512,1536]{1,0:T(8,128)S(1)}, u32[]{:S(2)}, u32[]{:S(2)}) collective-permute-start(f32[512,1536]{1,0:T(8,128)} %collective-permute-done.11.refs_12_), channel_id=1, source_target_pairs={{0,16},{1,49},{2,18},{3,51},{4,20},{5,53},{6,22},{7,55},{8,24},{9,... | collective-permute-start | bytes 9437192 | tf_op jit(solution)/shard_map/ppermute | solution.py:199
  168.2 40.6 %collective-permute-start.13 = (f32[512,1536]{1,0:T(8,128)}, f32[512,1536]{1,0:T(8,128)S(1)}, u32[]{:S(2)}, u32[]{:S(2)}) collective-permute-start(f32[512,1536]{1,0:T(8,128)} %collective-permute-done.10.refs_11_), channel_id=1, source_target_pairs={{0,2},{1,7},{2,4},{3,1},{4,6},{5,3},{6,0},{7,5},{8,10},{9,15},{10,... | collective-permute-start | bytes 9437192 | tf_op jit(solution)/shard_map/ppermute | solution.py:199
  169.7 39.1 %collective-permute-start.14 = (f32[512,1536]{1,0:T(8,128)}, f32[512,1536]{1,0:T(8,128)S(1)}, u32[]{:S(2)}, u32[]{:S(2)}) collective-permute-start(f32[512,1536]{1,0:T(8,128)} %collective-permute-done.4.refs_5_), channel_id=1, source_target_pairs={{0,8},{1,73},{2,10},{3,75},{4,12},{5,77},{6,14},{7,79},{8,64},{9,1... | collective-permute-start | bytes 9437192 | tf_op jit(solution)/shard_map/ppermute | solution.py:199
  173.0 3.8 copy-start.8
  208.7 4.5 %copy-start.9 = (f32[512,1536]{1,0:T(8,128)}, f32[512,1536]{1,0:T(8,128)S(1)}, u32[]{:S(2)}) copy-start(f32[512,1536]{1,0:T(8,128)S(1)} %collective-permute-done.12.refs_13_) | copy-start | bytes 9437188
  208.7 4.5 %copy-start.10 = (f32[512,1536]{1,0:T(8,128)}, f32[512,1536]{1,0:T(8,128)S(1)}, u32[]{:S(2)}) copy-start(f32[512,1536]{1,0:T(8,128)S(1)} %collective-permute-done.13.refs_14_) | copy-start | bytes 9437188
  208.9 8.3 %copy-start.11 = (f32[512,1536]{1,0:T(8,128)}, f32[512,1536]{1,0:T(8,128)S(1)}, u32[]{:S(2)}) copy-start(f32[512,1536]{1,0:T(8,128)S(1)} %collective-permute-done.14.refs_15_) | copy-start | bytes 9437188
  229.2 3.8 collective-permute-start.15
  229.4 6.6 %copy-start.2 = (f32[512,1536]{1,0:T(8,128)S(1)}, f32[512,1536]{1,0:T(8,128)}, u32[]{:S(2)}) copy-start(f32[512,1536]{1,0:T(8,128)} %copy-done.1) | copy-start | bytes 9437188
  229.4 6.6 %copy-start.5 = (f32[512,1536]{1,0:T(8,128)S(1)}, f32[512,1536]{1,0:T(8,128)}, u32[]{:S(2)}) copy-start(f32[512,1536]{1,0:T(8,128)} %copy-done.3) | copy-start | bytes 9437188
  262.4 7.6 %collective-permute-start.16 = (f32[64,128,128]{2,1,0:T(8,128)}, f32[64,128,128]{2,1,0:T(8,128)}, u32[]{:S(2)}, u32[]{:S(2)}) collective-permute-start(f32[64,128,128]{2,1,0:T(8,128)} %get-tuple-element.64), channel_id=1, source_target_pairs={{0,1},{1,0},{2,3},{3,2},{4,5},{5,4},{6,7},{7,6},{8,9},{9,8},{10,11... | collective-permute-start | bytes 12582920 | tf_op jit(solution)/shard_map/ppermute | solution.py:214
  274.7 114.2 %copy-start = (f32[8,2,8,128,128]{4,3,2,1,0:T(8,128)S(1)}, f32[8,2,8,128,128]{4,3,2,1,0:T(8,128)}, u32[]{:S(2)}) copy-start(f32[8,2,8,128,128]{4,3,2,1,0:T(8,128)} %constant_dynamic-update-slice_fusion) | copy-start | bytes 25165828
